TPU v7x, 128 devices: a whole 4x4x4 slice. The times are simulated.
128 devices in a mesh: row: 8 (over z, core), col: 16 (over x, y).
Axes of the slice: x: 4, y: 4, z: 4, core: 2. Of those that a mesh axis runs over, the one named last changes fastest.
Arguments:
- diag_inverse: float32 [1024, 1024], P(('row', 'col')), as said below
- row_basis: float32 [32, 128, 1024], P('row', 'col'), may hold values from -6 to 6
- row_coef: float32 [32, 128, 1024], P('row', 'col'), may hold values from -0.09375 to 0.09375
- row_ranks: int32 [32], P('row'), may hold values from 16 to 128, as said below
- col_basis: float32 [48, 128, 1024], P('col', 'row'), may hold values from -6 to 6
- col_coef: float32 [48, 128, 1024], P('col', 'row'), may hold values from -0.09375 to 0.09375
- col_ranks: int32 [48], P('col'), may hold values from 16 to 128, as said below
- tile_basis: float32 [32, 48, 1024, 128], P('row', 'col'), may hold values from -6 to 6
- tile_coef: float32 [32, 48, 1024, 128], P('row', 'col'), may hold values from -0.5 to 0.5
- tile_ranks: int32 [32, 48], P('row', 'col'), may hold values from 16 to 128, as said below
Outputs:
- new_basis: bfloat16 [32, 48, 1024, 128], P('row', 'col')
- new_coef: bfloat16 [32, 48, 1024, 128], P('row', 'col')
Inputs may be any that keep to these rules, and one draw needn't show every extreme that they name: `row_ranks`: rank of each panel tile; the smallest and largest values occur in every draw. `col_ranks`: rank of each panel tile; the smallest and largest values occur in every draw. `tile_ranks`: rank of each trailing tile; the smallest and largest values occur in every draw. `diag_inverse`: lower triangular with a positive diagonal.
All inputs are finite; a program needn't handle non-finite values.
Results may differ from a plain program's by a relative error of at most 0.001.
Values sent between devices are 32-bit elements; how exact they have to be, the bound alone decides.
No kernel may reach another device: no remote copies, remote signals or barrier semaphores. Data moves between devices by JAX's collectives and lax.ppermute only.
A program may use at most 128 MiB of HBM per device.

v0:
```python
import math

import jax
import jax.numpy as jnp
from jax import lax
from jax.sharding import PartitionSpec as P

HIGHEST = lax.Precision.HIGHEST


def small_inverse(gram_matrix, eye_block):
    factor = jnp.linalg.cholesky(gram_matrix)
    return jax.scipy.linalg.solve_triangular(factor, eye_block, lower=True)


def orthonormal_twice(sketch_block, rank_keep):
    rank_width = rank_keep.shape[-1]
    eye_one = jnp.eye(rank_width, dtype=jnp.float32)[None, :, :]
    eye_block = jnp.broadcast_to(eye_one, (sketch_block.shape[0], rank_width, rank_width))
    gram_matrix = jnp.einsum("tnr,tns->trs", sketch_block, sketch_block, precision=HIGHEST)
    gram_matrix = gram_matrix + eye_one * (1.0 - rank_keep)[:, None, :]
    first_inverse = small_inverse(gram_matrix, eye_block)
    half_gram = jnp.einsum("trs,tus->tru", gram_matrix, first_inverse, precision=HIGHEST)
    second_gram = jnp.einsum("trs,tsu->tru", first_inverse, half_gram, precision=HIGHEST)
    second_gram = 0.5 * (second_gram + jnp.swapaxes(second_gram, 1, 2))
    second_inverse = small_inverse(second_gram, eye_block)
    combined = jnp.einsum("trs,tsu->tru", second_inverse, first_inverse, precision=HIGHEST)
    return jnp.einsum("tnr,tsr->tns", sketch_block, combined, precision=HIGHEST)


def share_mask(panel_ranks, rank_share, position):
    columns = position * rank_share + jnp.arange(rank_share, dtype=jnp.int32)
    return (columns[None, :] < panel_ranks[:, None]).astype(jnp.float32)[:, :, None]


def solve_rows(inverse_factor, coef_rows):
    tile_count, rank_rows, order = coef_rows.shape
    flat_rows = coef_rows.reshape(tile_count * rank_rows, order)
    solved = jnp.dot(flat_rows, inverse_factor.T, precision=HIGHEST)
    return solved.reshape(tile_count, rank_rows, order)


def body(
    diag_inverse,
    row_basis,
    row_coef,
    row_ranks,
    col_basis,
    col_coef,
    col_ranks,
    tile_basis,
    tile_coef,
    tile_ranks,
):
    inverse_whole = lax.all_gather(diag_inverse, ("row", "col"), axis=0, tiled=True)
    row_keep = share_mask(row_ranks, row_basis.shape[1], lax.axis_index("col"))
    row_left = row_basis * row_keep
    row_send = row_coef * row_keep
    row_send = solve_rows(inverse_whole, row_send)
    row_left, row_solved = (
        lax.all_gather(row_left, "col", axis=1, tiled=True),
        lax.all_gather(row_send, "col", axis=1, tiled=True),
    )
    col_keep = share_mask(col_ranks, col_basis.shape[1], lax.axis_index("row"))
    col_left = col_basis * col_keep
    col_send = col_coef * col_keep
    col_send = solve_rows(inverse_whole, col_send)
    col_left, col_solved = (
        lax.all_gather(col_left, "row", axis=1, tiled=True),
        lax.all_gather(col_send, "row", axis=1, tiled=True),
    )
    local_rows, local_cols, order, rank_width = tile_basis.shape

    def pair_product(left_rows, right_rows):
        return jnp.dot(left_rows, right_rows.T, precision=HIGHEST)

    coupling = jax.vmap(jax.vmap(pair_product, in_axes=(None, 0)), in_axes=(0, None))(
        row_solved, col_solved
    )
    tile_count = local_rows * local_cols
    rank_keep = (
        jnp.arange(rank_width, dtype=jnp.int32)[None, None, :] < tile_ranks[:, :, None]
    ).astype(jnp.float32)
    masked_left = tile_basis * rank_keep[:, :, None, :]
    masked_right = tile_coef * rank_keep[:, :, None, :]

    def make_sketch(tile_left, tile_right, left_panel, pair_coupling, right_panel):
        inner_gram = jnp.dot(tile_right.T, tile_right, precision=HIGHEST)
        cross_term = jnp.dot(right_panel, tile_right, precision=HIGHEST)
        return jnp.dot(tile_left, inner_gram, precision=HIGHEST) - jnp.dot(
            left_panel.T, jnp.dot(pair_coupling, cross_term, precision=HIGHEST), precision=HIGHEST
        )

    sketch_inner = jax.vmap(make_sketch, in_axes=(0, 0, None, 0, 0))
    sketch = jax.vmap(sketch_inner, in_axes=(0, 0, 0, 0, None))(
        masked_left, masked_right, row_left, coupling, col_left
    )
    flat_keep = rank_keep.reshape(tile_count, rank_width)
    flat_sketch = sketch.reshape(tile_count, order, rank_width)
    ortho_basis = orthonormal_twice(flat_sketch, flat_keep).reshape(
        local_rows, local_cols, order, rank_width
    )

    def make_coef(tile_left, tile_right, left_panel, pair_coupling, right_panel, basis_block):
        first_part = jnp.dot(
            tile_right, jnp.dot(tile_left.T, basis_block, precision=HIGHEST), precision=HIGHEST
        )
        left_proj = jnp.dot(left_panel, basis_block, precision=HIGHEST)
        second_part = jnp.dot(
            right_panel.T, jnp.dot(pair_coupling.T, left_proj, precision=HIGHEST), precision=HIGHEST
        )
        return first_part - second_part

    coef_inner = jax.vmap(make_coef, in_axes=(0, 0, None, 0, 0, 0))
    new_coef = jax.vmap(coef_inner, in_axes=(0, 0, 0, 0, None, 0))(
        masked_left, masked_right, row_left, coupling, col_left, ortho_basis
    )
    scaled_basis = ortho_basis * math.sqrt(order)
    return (scaled_basis.astype(jnp.bfloat16), new_coef.astype(jnp.bfloat16))


def solution(mesh):
    placed = (
        P(("row", "col"), None),
        P("row", "col", None),
        P("row", "col", None),
        P("row"),
        P("col", "row", None),
        P("col", "row", None),
        P("col"),
        P("row", "col", None, None),
        P("row", "col", None, None),
        P("row", "col"),
    )
    return jax.shard_map(
        body,
        mesh=mesh,
        in_specs=placed,
        out_specs=(P("row", "col", None, None), P("row", "col", None, None)),
        check_vma=False,
    )
```

profile of v0, /device:TPU:0, one launch (start us, length us, event | category | flops | bytes accessed | tf_op | source)
XLA Modules:
  0.0 832.9 jit_solution(4603722570218747166)
XLA Ops:
  7.2 0.7 all-gather.8.cloned.1.call-update
  8.0 0.7 compare_convert_fusion
  8.7 1.7 broadcast_multiply_fusion
  10.5 70.0 %all-gather.8.cloned.1.call-done = f32[1024,1024]{1,0:T(8,128)} async-done(((f32[8,1024]{1,0:T(8,128)}), f32[1024,1024]{1,0:T(8,128)}) %all-gather.8.cloned.1.call-update) | async-done | bytes 4194320 | tf_op jit(solution)/shard_map/all_gather | solution.py:55
  80.5 7.0 fusion.13
  87.6 0.7 compare_convert_fusion.1
  88.3 6.9 fusion.15
  95.3 0.3 all-gather.6.cloned.1.call-start
  95.6 0.7 broadcast_multiply_fusion.1
  96.4 0.1 lt.74
  96.7 15.7 %fusion.11 = f32[4,3,128,128]{3,2,1,0:T(8,128)S(1)} fusion(f32[4,3,1024,128]{3,2,1,0:T(8,128)} %param.21, f32[4,3,128]{2,1,0:T(4,128)S(1)} %fusion.51), kind=kOutput, calls=%fused_computation.14 | convolution fusion | flops 2417491968 | bytes 7084032 | tf_op jit(solution)/shard_map/vmap(vmap())/dot_general | solution.py:88
  112.4 7.9 fusion.9
  120.3 11.4 %all-gather.12.cloned.1.call-done = f32[3,128,1024]{2,1,0:T(8,128)} async-done(((f32[3,16,1024]{2,1,0:T(8,128)}), f32[3,128,1024]{2,1,0:T(8,128)}) %all-gather.12.cloned.1.call-update) | async-done | bytes 1572880 | tf_op jit(solution)/shard_map/all_gather | solution.py:70
  131.7 1.9 copy.30
  133.6 45.0 %all-gather.10.cloned.1.call-done = f32[4,128,1024]{2,1,0:T(8,128)} async-done(((f32[4,8,1024]{2,1,0:T(8,128)}), f32[4,128,1024]{2,1,0:T(8,128)}) %all-gather.10.cloned.1.call-update) | async-done | bytes 2097168 | tf_op jit(solution)/shard_map/all_gather | solution.py:62
  178.7 5.0 fusion.24
  183.7 2.0 fusion.41
  185.7 39.2 %all-gather.6.cloned.1.call-done = f32[4,128,1024]{2,1,0:T(8,128)} async-done(((f32[4,8,1024]{2,1,0:T(8,128)}), f32[4,128,1024]{2,1,0:T(8,128)}) %all-gather.6.cloned.1.call-update) | async-done | bytes 2097168 | tf_op jit(solution)/shard_map/all_gather | solution.py:61
  224.9 7.3 fusion.26
  232.3 8.3 bitcast_subtract_fusion.1
  240.6 2.7 copy-done
  243.3 10.5 %convolution_add_fusion = f32[12,128,128]{1,2,0:T(8,128)S(1)} fusion(f32[12,1024,128]{2,1,0:T(8,128)S(1)} %bitcast.79, f32[12,128]{1,0:T(8,128)S(1)} %convert_subtract_fusion, f32[128,128]{0,1:T(8,128)S(1)} %fusion.50), kind=kOutput, calls=%fused_computation.33 | convolution fusion | flops 2416312320 | bytes 7149568 | tf_op jit(solution)/shard_map/tnr,tns->trs/dot_general | solution.py:20
  253.8 0.3 copy.35
  254.1 0.1 fusion.40
  254.2 141.1 %custom-call.8 = f32[12,128,128]{2,1,0:T(8,128)S(1)} custom-call(f32[12,128,128]{2,1,0:T(8,128)S(1)} %fusion.40), custom_call_target="Cholesky" | custom-call | tf_op jit(solution)/shard_map/jit(cholesky)/cholesky | solution.py:12
  395.3 0.1 compare_reduce_fusion.1
  395.4 0.2 select_bitcast_fusion.1
  395.6 118.5 %custom-call.9 = f32[12,1,128,128]{2,3,1,0:T(8,128)} custom-call(f32[12,1,128,128]{3,2,1,0:T(8,128)S(1)} %select_bitcast_fusion.1), custom_call_target="InvertDiagBlocksLowerTriangular" | custom-call | tf_op jit(solution)/shard_map/jit(_solve_triangular)/vmap()/triangular_solve | solution.py:13
  514.1 2.5 fusion.38
  516.7 1.4 fusion.52
  518.1 0.9 fusion.53
  519.0 1.1 copy.39
  520.2 1.2 fusion.37
  521.4 0.3 copy.40
  521.7 1.0 fusion.36
  522.6 141.6 %custom-call.10 = f32[12,128,128]{2,1,0:T(8,128)S(1)} custom-call(f32[12,128,128]{2,1,0:T(8,128)} %fusion.36), custom_call_target="Cholesky" | custom-call | tf_op jit(solution)/shard_map/jit(cholesky)/cholesky | solution.py:12
  664.3 0.1 compare_reduce_fusion
  664.4 0.2 select_bitcast_fusion
  664.6 117.9 %custom-call.11 = f32[12,1,128,128]{2,3,1,0:T(8,128)S(1)} custom-call(f32[12,1,128,128]{3,2,1,0:T(8,128)S(1)} %select_bitcast_fusion), custom_call_target="InvertDiagBlocksLowerTriangular" | custom-call | tf_op jit(solution)/shard_map/jit(_solve_triangular)/vmap()/triangular_solve | solution.py:13
  782.5 1.4 fusion.34
  783.9 0.9 fusion.54
  784.8 8.5 %fusion.55 = f32[12,1024,128]{2,1,0:T(8,128)S(1)} fusion(f32[12,1024,128]{2,1,0:T(8,128)} %bitcast.80, f32[12,128,128]{2,1,0:T(8,128)S(1)} %fusion.54), kind=kOutput, calls=%fused_computation.78 | convolution fusion | flops 2415919104 | bytes 13369344 | tf_op jit(solution)/shard_map/tnr,tsr->tns/dot_general | solution.py:28
  793.3 10.4 %fusion.3 = f32[4,3,128,128]{3,2,1,0:T(8,128)S(1)} fusion(f32[4,3,1024,128]{3,2,1,0:T(8,128)S(1)} %bitcast.81, f32[4,3,1024,128]{3,2,1,0:T(8,128)S(1)} %bitcast.87, f32[4,3,128]{2,1,0:T(4,128)S(1)} %fusion.51), kind=kOutput, calls=%fused_computation.6 | convolution fusion | flops 2417491968 | bytes 13375488 | tf_op jit(solution)/shard_map/vmap(vmap())/dot_general | solution.py:106
  803.7 2.4 multiply_convert_fusion
  806.1 4.8 fusion.1
  810.9 1.5 fusion.32
  812.4 6.6 fusion.7
  819.0 7.2 fusion
  (37 shorter events, 0.6 us)
Async XLA Ops:
  7.2 88.5 %copy-start.3 = (f32[4,8,1024]{2,1,0:T(8,128)S(1)}, f32[4,8,1024]{2,1,0:T(8,128)}, u32[]{:S(2)}) copy-start(f32[4,8,1024]{2,1,0:T(8,128)} %param.14) | copy-start | bytes 393220
  7.2 89.2 %copy-start.4 = (s32[4,3]{1,0:T(4,128)S(1)}, s32[4,3]{1,0:T(4,128)}, u32[]{:S(2)}) copy-start(s32[4,3]{1,0:T(4,128)} %param.22) | copy-start | bytes 148
  7.2 73.3 %all-gather.8.cloned.1.call-start = ((), (), s32[]{:S(2)}) async-start(), calls=%async_computation.1 | async-start | bytes 4227072 | tf_op jit(solution)/shard_map/all_gather | solution.py:55
  7.9 104.5 %all-gather.14.cloned.1.call-start = ((), (), s32[]{:S(2)}) async-start(), calls=%async_computation.4 | async-start | bytes 1769472 | tf_op jit(solution)/shard_map/all_gather | solution.py:69
  10.4 121.3 %all-gather.12.cloned.1.call-start = ((), (), s32[]{:S(2)}) async-start(), calls=%async_computation.3 | async-start | bytes 1769472 | tf_op jit(solution)/shard_map/all_gather | solution.py:70
  87.5 91.1 %all-gather.10.cloned.1.call-start = ((), (), s32[]{:S(2)}) async-start(), calls=%async_computation.2 | async-start | bytes 2228224 | tf_op jit(solution)/shard_map/all_gather | solution.py:62
  95.3 129.6 %all-gather.6.cloned.1.call-start = ((), (), s32[]{:S(2)}) async-start(), calls=%async_computation | async-start | bytes 2228224 | tf_op jit(solution)/shard_map/all_gather | solution.py:61
  240.6 2.7 copy-start
  783.9 9.4 %slice-start.2 = ((s8[6291456]{0:T(1024)(128)(4,1)}), s8[4194304]{0:T(1024)(128)(4,1)S(1)}, s32[]{:S(2)}) async-start(s8[6291456]{0:T(1024)(128)(4,1)} %bitcast.86), calls=%async_computation.7 | async-start | bytes 8388608
  784.8 8.5 %slice-start.3 = ((s8[6291456]{0:T(1024)(128)(4,1)}), s8[2097152]{0:T(1024)(128)(4,1)S(1)}, s32[]{:S(2)}) async-start(s8[6291456]{0:T(1024)(128)(4,1)} %bitcast.86), calls=%async_computation.8 | async-start | bytes 4194304
  803.7 2.4 copy-start.1
  803.7 8.7 %slice-start = ((s8[6291456]{0:T(1024)(128)(4,1)}), s8[2097152]{0:T(1024)(128)(4,1)S(1)}, s32[]{:S(2)}) async-start(s8[6291456]{0:T(1024)(128)(4,1)} %bitcast.84), calls=%async_computation.5 | async-start | bytes 4194304
  806.1 6.3 slice-start.1
  812.4 6.6 copy-start.2
Sparse Core Ops, SparseCore 0:
  11.1 69.3 all-gather.7
  82.8 22.0 all-gather.13
  107.1 24.5 all-gather.11
  133.8 44.8 all-gather.9
  180.7 44.1 all-gather.5
where the time goes:
time: 838 us; the launch traced here: 833 us
  other arithmetic  528 us (63%)
  waiting for transfers between devices  166 us (20%)
  matrix products  117 us (14%)
  between operations  14.3 us (2%)
    another operation x7, other arithmetic, small_inverse(): factor = jnp.linalg.cholesky(gram_matrix)  283 us
    another operation x5, other arithmetic, small_inverse(): return jax.scipy.linalg.solve_triangular(factor, eye_block, lower=True)  237 us
    all_gather x1, waiting for transfers between devices, body(): lax.all_gather(diag_inverse, ('row', 'col'), axis=0, tiled=True)  70 us
    all_gather x1, waiting for transfers between devices, body(): lax.all_gather(row_send, 'col', axis=1, tiled=True)  45 us
    all_gather x1, waiting for transfers between devices, body(): lax.all_gather(row_left, 'col', axis=1, tiled=True)  39.2 us
  transfers between devices with their start and end apart: 5, of which 4 were waited for; matrix products, arithmetic and copies ran while one was open for 6% of the time, Pallas kernels for 0%

commit v1 on v0

--- a/solution.py
+++ b/solution.py
@@ -3,28 +3,98 @@
 import jax
 import jax.numpy as jnp
 from jax import lax
+from jax.experimental import pallas as pl
+from jax.experimental.pallas import tpu as pltpu
 from jax.sharding import PartitionSpec as P
 
 HIGHEST = lax.Precision.HIGHEST
 
 
-def small_inverse(gram_matrix, eye_block):
-    factor = jnp.linalg.cholesky(gram_matrix)
-    return jax.scipy.linalg.solve_triangular(factor, eye_block, lower=True)
+BF = jnp.bfloat16
+F32 = jnp.float32
+BLK = 32
+
+def split3(a):
+    h = a.astype(BF)
+    rest = a - h.astype(F32)
+    m = rest.astype(BF)
+    l = (rest - m.astype(F32)).astype(BF)
+    return h, m, l
+
+def dot6(a, b, ca, cb):
+    ah, am, al = split3(a)
+    bh, bm, bl = split3(b)
+    lhs = jnp.concatenate([ah, ah, am, ah, al, am], axis=ca)
+    rhs = jnp.concatenate([bh, bm, bh, bl, bh, bm], axis=cb)
+    return lax.dot_general(lhs, rhs, (((ca,), (cb,)), ((), ())), preferred_element_type=F32)
+
+def eliminate(block, base, lanes, rows):
+    groups = BLK // 8
+    parts = [block[8 * g:8 * g + 8] for g in range(groups)]
+    done = [jnp.zeros((8, 128), F32)] * groups
+    for kk in range(BLK):
+        g0, s = kk // 8, kk % 8
+        k = base + kk
+        at_k = lanes == k
+        cols = [parts[g][:, k:k + 1] for g in range(g0, groups)]
+        scale = lax.rsqrt(cols[0][s:s + 1, :])
+        row = jnp.where(at_k[0:1], 1.0, parts[g0][s:s + 1, :]) * scale
+        for g in range(g0, groups):
+            col = cols[g - g0] * scale
+            if g == g0:
+                keep = jnp.where(at_k, 0.0, parts[g])
+                new = keep - col * row
+                parts[g] = jnp.where(rows > s, new, jnp.where(rows == s, row, parts[g]))
+            else:
+                parts[g] = jnp.where(at_k, 0.0, parts[g]) - col * row
+    return jnp.concatenate(parts, axis=0)
+
+def inverse_factor(work, tiles):
+    lanes = lax.broadcasted_iota(jnp.int32, (8, 128), 1)
+    rows = lax.broadcasted_iota(jnp.int32, (8, 128), 0)
+    lane_b = lax.broadcasted_iota(jnp.int32, (BLK, 128), 1)
+    row_b = lax.broadcasted_iota(jnp.int32, (BLK, 128), 0)
+    for t in range(128 // BLK):
+        base = t * BLK
+        for m in range(tiles):
+            r = eliminate(work[m, base:base + BLK, :], base, lanes, rows)
+            inside = (lane_b >= base) & (lane_b < base + BLK)
+            r = jnp.where(inside & (lane_b - base > row_b), 0.0, r)
+            if base + BLK < 128:
+                upd = dot6(r, r, 0, 0)
+                rest = work[m, base + BLK:, :]
+                lane_r = lax.broadcasted_iota(jnp.int32, rest.shape, 1)
+                rest = jnp.where((lane_r >= base) & (lane_r < base + BLK), 0.0, rest)
+                work[m, base + BLK:, :] = rest - upd[base + BLK:, :]
+            work[m, base:base + BLK, :] = jnp.where(lane_b - base > row_b, 0.0, r)
+
+def chol_kernel(g_ref, o_ref, work):
+    tiles = g_ref.shape[0]
+    for m in range(tiles):
+        work[m] = g_ref[m]
+    inverse_factor(work, tiles)
+    for m in range(tiles):
+        first = work[m]
+        o_ref[m] = first
+        second = dot6(first, dot6(g_ref[m], first, 1, 1), 1, 0)
+        work[m] = 0.5 * (second + second.T)
+    inverse_factor(work, tiles)
+    for m in range(tiles):
+        o_ref[m] = dot6(work[m], o_ref[m], 1, 0)
+
+def chol2(g):
+    return pl.pallas_call(chol_kernel, out_shape=jax.ShapeDtypeStruct(g.shape, F32),
+        in_specs=[pl.BlockSpec(memory_space=pltpu.VMEM)], out_specs=pl.BlockSpec(memory_space=pltpu.VMEM),
+        scratch_shapes=[pltpu.VMEM(g.shape, F32)],
+        compiler_params=pltpu.CompilerParams(vmem_limit_bytes=48*2**20), name="chol2")(g)
 
 
 def orthonormal_twice(sketch_block, rank_keep):
     rank_width = rank_keep.shape[-1]
     eye_one = jnp.eye(rank_width, dtype=jnp.float32)[None, :, :]
-    eye_block = jnp.broadcast_to(eye_one, (sketch_block.shape[0], rank_width, rank_width))
     gram_matrix = jnp.einsum("tnr,tns->trs", sketch_block, sketch_block, precision=HIGHEST)
     gram_matrix = gram_matrix + eye_one * (1.0 - rank_keep)[:, None, :]
-    first_inverse = small_inverse(gram_matrix, eye_block)
-    half_gram = jnp.einsum("trs,tus->tru", gram_matrix, first_inverse, precision=HIGHEST)
-    second_gram = jnp.einsum("trs,tsu->tru", first_inverse, half_gram, precision=HIGHEST)
-    second_gram = 0.5 * (second_gram + jnp.swapaxes(second_gram, 1, 2))
-    second_inverse = small_inverse(second_gram, eye_block)
-    combined = jnp.einsum("trs,tsu->tru", second_inverse, first_inverse, precision=HIGHEST)
+    combined = chol2(gram_matrix)
     return jnp.einsum("tnr,tsr->tns", sketch_block, combined, precision=HIGHEST)
 
 

time: 838 us -> 329 us (0.39)
  other arithmetic: 528 us -> 6.4 us
  Pallas kernels: 0 us -> 27.8 us
  matrix products: 117 us -> 106 us
    another operation x12 -> x0, other arithmetic: 520 us -> none  [the longest x7 283 us: small_inverse(): factor = jnp.linalg.cholesky(gram_matrix)]
    pallas_call x0 -> x1, Pallas kernels: none -> 27.8 us  [chol2(): pl.pallas_call(chol_kernel, out_shape=jax.ShapeDtypeStruct(g.shape, F32),...]
  transfers between devices with their start and end apart: 5 -> 5, of which waited for: 4 -> 4; matrix products, arithmetic and copies ran while one was open for 6% -> 16% of each run, Pallas kernels for 0% -> 0%
where the time goes in v1:
time: 329 us; the launch traced here: 324 us
  waiting for transfers between devices  166 us (50%)
  matrix products  106 us (32%)
  Pallas kernels  27.8 us (8%)
  between operations  14.2 us (4%)
  other arithmetic  6.4 us (2%)
    all_gather x1, waiting for transfers between devices, body(): lax.all_gather(diag_inverse, ('row', 'col'), axis=0, tiled=True)  70 us
    all_gather x1, waiting for transfers between devices, body(): lax.all_gather(row_send, 'col', axis=1, tiled=True)  45 us
    all_gather x1, waiting for transfers between devices, body(): lax.all_gather(row_left, 'col', axis=1, tiled=True)  39.2 us
    pallas_call x1, Pallas kernels, chol2(): pl.pallas_call(chol_kernel, out_shape=jax.ShapeDtypeStruct(g.shape, F32),...  27.8 us
    dot_general x1, matrix products, make_sketch(): inner_gram = jnp.dot(tile_right.T, tile_right, precision=HIGHEST)  15.7 us
    dot_general x2, matrix products, solve_rows(): solved = jnp.dot(flat_rows, inverse_factor.T, precision=HIGHEST)  13.9 us
    all_gather x1, waiting for transfers between devices, body(): lax.all_gather(col_send, 'row', axis=1, tiled=True)  11.4 us
    dot_general x1, matrix products, make_coef(): jnp.dot(tile_left.T, basis_block, precision=HIGHEST)  10.7 us
  transfers between devices with their start and end apart: 5, of which 4 were waited for; matrix products, arithmetic and copies ran while one was open for 16% of the time, Pallas kernels for 0%

profile of v1, /device:TPU:0, one launch (start us, length us, event | category | flops | bytes accessed | tf_op | source)
XLA Modules:
  0.0 323.5 jit_solution(7009230325103637880)
XLA Ops:
  7.2 0.0 copy-start.2
  7.2 0.0 copy-start.3
  7.2 0.0 all-gather.8.cloned.1.call-start
  7.2 0.7 all-gather.8.cloned.1.call-update
  7.9 0.0 all-gather.14.cloned.1.call-start
  8.0 0.7 compare_convert_fusion
  8.7 1.7 broadcast_multiply_fusion.1
  10.4 0.0 all-gather.14.cloned.1.call-update
  10.4 0.0 all-gather.12.cloned.1.call-start
  10.5 70.0 %all-gather.8.cloned.1.call-done = f32[1024,1024]{1,0:T(8,128)} async-done(((f32[8,1024]{1,0:T(8,128)}), f32[1024,1024]{1,0:T(8,128)}) %all-gather.8.cloned.1.call-update) | async-done | bytes 4194320 | tf_op jit(solution)/shard_map/all_gather | solution.py:125
  80.5 7.0 %fusion.7 = f32[3,16,1024]{2,1,0:T(8,128)} fusion(f32[1024,1024]{1,0:T(8,128)} %all-gather.8.cloned.1.call-done, f32[3,16,1024]{2,1,0:T(8,128)} %param.15, f32[3,16]{1,0:T(4,128)S(1)} %compare_convert_fusion), kind=kOutput, calls=%fused_computation.10 | convolution fusion | flops 604028928 | bytes 4587712 | tf_op jit(solution)/shard_map/dot_general | solution.py:109
  87.5 0.0 all-gather.12.cloned.1.call-update
  87.5 0.0 all-gather.10.cloned.1.call-start
  87.6 0.7 compare_convert_fusion.1
  88.3 6.9 %fusion.9 = f32[4,8,1024]{2,1,0:T(8,128)} fusion(f32[1024,1024]{1,0:T(8,128)} %all-gather.8.cloned.1.call-done, f32[4,8,1024]{2,1,0:T(8,128)} %param.12, f32[4,8]{1,0:T(4,128)S(1)} %compare_convert_fusion.1), kind=kOutput, calls=%fused_computation.12 | convolution fusion | flops 402685952 | bytes 4456576 | tf_op jit(solution)/shard_map/dot_general | solution.py:109
  95.2 0.0 all-gather.10.cloned.1.call-update
  95.3 0.3 all-gather.6.cloned.1.call-start
  95.6 0.0 copy-done.2
  95.6 0.7 broadcast_multiply_fusion.2
  96.4 0.0 all-gather.6.cloned.1.call-update
  96.4 0.1 lt.74
  96.5 0.1 convert_subtract_fusion
  96.6 0.1 fusion.37
  96.6 15.7 %fusion.38 = f32[4,3,128,128]{3,2,1,0:T(8,128)S(1)} fusion(f32[4,3,1024,128]{3,2,1,0:T(8,128)} %param.18, f32[4,3,128]{2,1,0:T(4,128)S(1)} %fusion.37), kind=kOutput, calls=%fused_computation.51 | convolution fusion | flops 2419064832 | bytes 7084032 | tf_op jit(solution)/shard_map/vmap(vmap())/dot_general | solution.py:158
  112.4 0.0 all-gather.14.cloned.1.call-done
  112.4 7.9 %fusion.1 = f32[3,128,4,128]{3,1,2,0:T(8,128)} fusion(f32[3,128,1024]{2,1,0:T(8,128)} %all-gather.14.cloned.1.call-done, f32[4,3,1024,128]{3,2,1,0:T(8,128)} %param.18, f32[4,3,128]{2,1,0:T(4,128)S(1)} %fusion.37), kind=kOutput, calls=%fused_computation.3 | convolution fusion | flops 2417491968 | bytes 8656896 | tf_op jit(solution)/shard_map/vmap(vmap())/dot_general | solution.py:159
  120.3 11.4 %all-gather.12.cloned.1.call-done = f32[3,128,1024]{2,1,0:T(8,128)} async-done(((f32[3,16,1024]{2,1,0:T(8,128)}), f32[3,128,1024]{2,1,0:T(8,128)}) %all-gather.12.cloned.1.call-update) | async-done | bytes 1572880 | tf_op jit(solution)/shard_map/all_gather | solution.py:140
  131.7 1.9 copy.13
  133.6 45.0 %all-gather.10.cloned.1.call-done = f32[4,128,1024]{2,1,0:T(8,128)} async-done(((f32[4,8,1024]{2,1,0:T(8,128)}), f32[4,128,1024]{2,1,0:T(8,128)}) %all-gather.10.cloned.1.call-update) | async-done | bytes 2097168 | tf_op jit(solution)/shard_map/all_gather | solution.py:132
  178.7 5.0 %fusion.15 = f32[4,128,3,128]{3,1,2,0:T(8,128)S(1)} fusion(f32[4,128,1024]{2,1,0:T(8,128)} %all-gather.10.cloned.1.call-done, f32[3,128,1024]{1,2,0:T(8,128)S(1)} %copy.13), kind=kOutput, calls=%fused_computation.17 | convolution fusion | flops 2415919104 | bytes 4456448 | tf_op jit(solution)/shard_map/vmap(vmap())/dot_general | solution.py:145
  183.7 2.0 fusion.27
  185.7 39.2 %all-gather.6.cloned.1.call-done = f32[4,128,1024]{2,1,0:T(8,128)} async-done(((f32[4,8,1024]{2,1,0:T(8,128)}), f32[4,128,1024]{2,1,0:T(8,128)}) %all-gather.6.cloned.1.call-update) | async-done | bytes 2097168 | tf_op jit(solution)/shard_map/all_gather | solution.py:131
  224.9 7.3 %fusion.19 = f32[4,1024,3,128]{3,1,2,0:T(8,128)S(1)} fusion(f32[4,3,128,128]{3,2,1,0:T(8,128)S(1)} %fusion.27, f32[4,128,1024]{2,1,0:T(8,128)} %all-gather.6.cloned.1.call-done), kind=kOutput, calls=%fused_computation.21 | convolution fusion | flops 2415919104 | bytes 9175040 | tf_op jit(solution)/shard_map/vmap(vmap())/dot_general | solution.py:160
  232.3 8.1 %bitcast_subtract_fusion.1 = f32[4,3,1024,128]{3,2,1,0:T(8,128)S(1)} fusion(f32[4,1024,3,128]{3,1,2,0:T(8,128)S(1)} %fusion.19, f32[4,3,128,128]{3,2,1,0:T(8,128)S(1)} %fusion.38, f32[4,3,1024,128]{3,2,1,0:T(8,128)} %param.17, f32[4,3,128]{2,1,0:T(4,128)S(1)} %fusion.37), kind=kOutput, calls=%fused_computation.2 | convolution fusion | flops 2419064832 | bytes 19666944 | tf_op jit(solution)/shard_map/vmap(vmap())/dot_general | solution.py:160
  240.3 10.0 %convolution_add_fusion.g_ref = f32[12,128,128]{2,1,0:T(8,128)S(1)} fusion(f32[12,1024,128]{2,1,0:T(8,128)S(1)} %bitcast.58, f32[12,128]{1,0:T(8,128)S(1)} %convert_subtract_fusion, f32[128,128]{1,0:T(8,128)S(1)} %fusion.36), kind=kOutput, calls=%fused_computation.27 | convolution fusion | flops 2416312320 | bytes 7149568 | tf_op jit(solution)/shard_map/tnr,tns->trs/dot_general | solution.py:95
  250.4 0.0 slice-start.2
  250.4 27.8 %chol2.1 = f32[12,128,128]{2,1,0:T(8,128)S(1)} custom-call(f32[12,128,128]{2,1,0:T(8,128)S(1)} %convolution_add_fusion.g_ref), custom_call_target="tpu_custom_call" | custom-call | tf_op jit(solution)/shard_map/chol2/pallas_call | solution.py:86
  278.2 0.0 slice-start.3
  278.2 6.4 %fusion.39 = f32[12,1024,128]{2,1,0:T(8,128)S(1)} fusion(f32[12,1024,128]{2,1,0:T(8,128)S(1)} %bitcast.59, f32[12,128,128]{2,1,0:T(8,128)S(1)} %chol2.1), kind=kOutput, calls=%fused_computation.52 | convolution fusion | flops 2415919104 | bytes 13369344 | tf_op jit(solution)/shard_map/tnr,tsr->tns/dot_general | solution.py:98
  284.6 10.7 %fusion.3 = f32[4,3,128,128]{3,2,1,0:T(8,128)S(1)} fusion(f32[4,3,1024,128]{3,2,1,0:T(8,128)S(1)} %bitcast.60, f32[4,3,1024,128]{3,2,1,0:T(8,128)S(1)} %bitcast.64, f32[4,3,128]{2,1,0:T(4,128)S(1)} %fusion.37), kind=kOutput, calls=%fused_computation.6 | convolution fusion | flops 2417491968 | bytes 13375488 | tf_op jit(solution)/shard_map/vmap(vmap())/dot_general | solution.py:176
  295.4 0.0 copy-start
  295.4 2.4 multiply_convert_fusion
  297.7 0.0 copy-done
  297.8 4.4 %fusion.17 = f32[4,128,3,128]{3,1,2,0:T(8,128)S(1)} fusion(f32[4,3,1024,128]{3,2,1,0:T(8,128)S(1)} %bitcast.62, f32[4,128,1024]{2,1,0:T(8,128)S(1)} %copy-done), kind=kOutput, calls=%fused_computation.19 | convolution fusion | flops 2415919104 | bytes 9175040 | tf_op jit(solution)/shard_map/vmap(vmap())/dot_general | solution.py:178
  302.2 0.0 slice-start.1
  302.2 1.5 fusion.25
  303.6 5.5 %fusion.23 = f32[3,1024,4,128]{3,1,0,2:T(8,128)S(1)} fusion(f32[3,128,1024]{2,1,0:T(8,128)S(1)} %copy-done.1, f32[4,3,128,128]{3,2,0,1:T(8,128)S(1)} %fusion.25), kind=kOutput, calls=%fused_computation.25 | convolution fusion | flops 2415919104 | bytes 8650752 | tf_op jit(solution)/shard_map/vmap(vmap())/dot_general | solution.py:179
  309.2 7.6 %fusion = bf16[4,3,1024,128]{3,2,1,0:T(8,128)(2,1)} fusion(f32[3,1024,4,128]{3,1,0,2:T(8,128)S(1)} %fusion.23, f32[4,3,128,128]{3,2,1,0:T(8,128)S(1)} %fusion.3, f32[4,3,1024,128]{3,2,1,0:T(8,128)S(1)} %bitcast.57, f32[4,3,128]{2,1,0:T(4,128)S(1)} %fusion.37), kind=kOutput, calls=%fused_computation.1 | convolution fusion | flops 2420637696 | bytes 16521216 | tf_op jit(solution)/shard_map/vmap(vmap())/dot_general | solution.py:175
  (13 shorter events, 0.0 us)
Async XLA Ops:
  7.2 88.4 %copy-start.2 = (f32[4,8,1024]{2,1,0:T(8,128)S(1)}, f32[4,8,1024]{2,1,0:T(8,128)}, u32[]{:S(2)}) copy-start(f32[4,8,1024]{2,1,0:T(8,128)} %param.11) | copy-start | bytes 393220
  7.2 89.2 %copy-start.3 = (s32[4,3]{1,0:T(4,128)S(1)}, s32[4,3]{1,0:T(4,128)}, u32[]{:S(2)}) copy-start(s32[4,3]{1,0:T(4,128)} %param.19) | copy-start | bytes 148
  7.2 73.3 %all-gather.8.cloned.1.call-start = ((), (), s32[]{:S(2)}) async-start(), calls=%async_computation.1 | async-start | bytes 4227072 | tf_op jit(solution)/shard_map/all_gather | solution.py:125
  7.9 104.5 %all-gather.14.cloned.1.call-start = ((), (), s32[]{:S(2)}) async-start(), calls=%async_computation.4 | async-start | bytes 1769472 | tf_op jit(solution)/shard_map/all_gather | solution.py:139
  10.4 121.3 %all-gather.12.cloned.1.call-start = ((), (), s32[]{:S(2)}) async-start(), calls=%async_computation.3 | async-start | bytes 1769472 | tf_op jit(solution)/shard_map/all_gather | solution.py:140
  87.5 91.1 %all-gather.10.cloned.1.call-start = ((), (), s32[]{:S(2)}) async-start(), calls=%async_computation.2 | async-start | bytes 2228224 | tf_op jit(solution)/shard_map/all_gather | solution.py:132
  95.3 129.7 %all-gather.6.cloned.1.call-start = ((), (), s32[]{:S(2)}) async-start(), calls=%async_computation | async-start | bytes 2228224 | tf_op jit(solution)/shard_map/all_gather | solution.py:131
  250.4 34.3 %slice-start.2 = ((s8[6291456]{0:T(1024)(128)(4,1)}), s8[4194304]{0:T(1024)(128)(4,1)S(1)}, s32[]{:S(2)}) async-start(s8[6291456]{0:T(1024)(128)(4,1)} %bitcast.63), calls=%async_computation.7 | async-start | bytes 8388608
  278.2 6.4 %slice-start.3 = ((s8[6291456]{0:T(1024)(128)(4,1)}), s8[2097152]{0:T(1024)(128)(4,1)S(1)}, s32[]{:S(2)}) async-start(s8[6291456]{0:T(1024)(128)(4,1)} %bitcast.63), calls=%async_computation.8 | async-start | bytes 4194304
  295.4 2.4 copy-start
  297.7 5.9 %copy-start.1 = (f32[3,128,1024]{2,1,0:T(8,128)S(1)}, f32[3,128,1024]{2,1,0:T(8,128)}, u32[]{:S(2)}) copy-start(f32[3,128,1024]{2,1,0:T(8,128)} %all-gather.14.cloned.1.call-done) | copy-start | bytes 4718596
  297.7 11.5 %slice-start = ((s8[6291456]{0:T(1024)(128)(4,1)}), s8[4194304]{0:T(1024)(128)(4,1)S(1)}, s32[]{:S(2)}) async-start(s8[6291456]{0:T(1024)(128)(4,1)} %bitcast.56), calls=%async_computation.5 | async-start | bytes 8388608
  302.2 7.1 %slice-start.1 = ((s8[6291456]{0:T(1024)(128)(4,1)}), s8[2097152]{0:T(1024)(128)(4,1)S(1)}, s32[]{:S(2)}) async-start(s8[6291456]{0:T(1024)(128)(4,1)} %bitcast.56), calls=%async_computation.6 | async-start | bytes 4194304
Sparse Core Ops, SparseCore 0:
  11.1 69.3 all-gather.7
  82.8 22.0 all-gather.13
  107.1 24.5 all-gather.11
  133.8 44.8 all-gather.9
  180.7 44.1 all-gather.5
